TPU v7x, 256 devices: a whole 4x4x8 slice. The times are simulated.
256 devices in a mesh: seq: 64 (over z, x, y_lo), ch: 4 (over y_hi, core).
Axes of the slice: x: 4, y: 4 (y_hi: 2, y_lo: 2; y = y_hi * 2 + y_lo), z: 8, core: 2. Of those that a mesh axis runs over, the one named last changes fastest.
Arguments:
- stream: bfloat16 [1, 768, 262144], P(None, 'ch', 'seq'), may hold values from -40 to 40
- in_weight: float32 [768], P('ch'), may hold values from -4 to 4
- in_bias: float32 [768], P('ch'), may hold values from -2 to 2
- out_weight: float32 [768], P('ch'), may hold values from -4 to 4
- out_bias: float32 [768], P('ch'), may hold values from -2 to 2
- first_mix: bfloat16 [512, 512], replicated, may hold values from -0.25 to 0.25
- twist_in: bfloat16 [512, 512], P(None, 'seq'), may hold values from -4 to 4
- second_mix: bfloat16 [512, 512], replicated, may hold values from -0.25 to 0.25
- kernel: bfloat16 [768, 512, 512], P('ch', 'seq'), may hold values from -4 to 4
- third_mix: bfloat16 [512, 512], replicated, may hold values from -0.25 to 0.25
- twist_out: bfloat16 [512, 512], P(None, 'seq'), may hold values from -4 to 4
- fourth_mix: bfloat16 [512, 512], replicated, may hold values from -0.25 to 0.25
- norm_gain: bfloat16 [768], replicated, may hold values from 0.5 to 2
- gate_weight: bfloat16 [4, 192, 768], replicated, may hold values from -0.4375 to 0.4375
- up_weight: bfloat16 [4, 192, 768], replicated, may hold values from -0.4375 to 0.4375
- down_weight: bfloat16 [4, 192, 768], replicated, may hold values from -0.21875 to 0.21875
Outputs:
- layer_out: bfloat16 [1, 768, 262144], P(None, 'ch', 'seq')
All inputs are finite; a program needn't handle non-finite values.
Results may differ from a plain program's by a relative error of at most 0.012.
Values may be sent and summed in bfloat16 or wider, within the bound.
A program may use at most 192 MiB of HBM per device.

v0:
```python
import jax
import jax.numpy as jnp
from jax import lax
from jax.sharding import PartitionSpec as P

epsilon = 1e-05


def to_wide(array_in):
    return array_in.astype(jnp.float32)


def local(
    stream,
    in_weight,
    in_bias,
    out_weight,
    out_bias,
    first_mix,
    twist_in,
    second_mix,
    kernel,
    third_mix,
    twist_out,
    fourth_mix,
    norm_gain,
    gate_weight,
    up_weight,
    down_weight,
):
    seqs_dev, width_dev, tokens_dev = stream.shape
    rows_dev = kernel.shape[1]
    line_length = kernel.shape[2]
    source = to_wide(stream)
    gated_in = (source * jax.nn.sigmoid(source * in_weight[:, None] + in_bias[:, None])).astype(
        jnp.bfloat16
    )
    gated_four = gated_in.reshape(seqs_dev, width_dev, rows_dev, line_length)
    line_data, kernel_lines = (
        lax.all_to_all(gated_four, "seq", split_axis=1, concat_axis=2, tiled=True),
        lax.all_to_all(kernel[None], "seq", split_axis=1, concat_axis=2, tiled=True),
    )
    table_in, table_out = (
        lax.all_gather(twist_in, "seq", axis=1, tiled=True),
        lax.all_gather(twist_out, "seq", axis=1, tiled=True),
    )
    few_channels = line_data.shape[1]
    full_rows = line_data.shape[2]
    batch_lines = line_data.reshape(seqs_dev * few_channels, full_rows, line_length)
    first_value = jnp.matmul(first_mix, batch_lines, preferred_element_type=jnp.float32)
    section_one = (first_value * to_wide(table_in)).astype(jnp.bfloat16)
    second_value = jnp.einsum(
        "baj,ej->bae", section_one, second_mix, preferred_element_type=jnp.float32
    )
    second_value = second_value.reshape(seqs_dev, few_channels, full_rows, line_length)
    section_two = (second_value * to_wide(kernel_lines[0])[None]).astype(jnp.bfloat16)
    section_two = section_two.reshape(seqs_dev * few_channels, full_rows, line_length)
    third_value = jnp.einsum(
        "bae,ge->bag", section_two, third_mix, preferred_element_type=jnp.float32
    )
    section_three = lax.optimization_barrier(third_value.astype(jnp.bfloat16))
    twisted = (to_wide(section_three) * to_wide(table_out)).astype(jnp.bfloat16)
    returned = jnp.matmul(fourth_mix, twisted, preferred_element_type=jnp.float32).astype(
        jnp.bfloat16
    )
    returned = returned.reshape(seqs_dev, few_channels, full_rows, line_length)
    at_home = lax.all_to_all(returned, "seq", split_axis=2, concat_axis=1, tiled=True)
    at_home = at_home.reshape(seqs_dev, width_dev, tokens_dev)
    mixed_out = (
        source + to_wide(at_home) * jax.nn.sigmoid(source * out_weight[:, None] + out_bias[:, None])
    ).astype(jnp.bfloat16)
    my_block = lax.axis_index("ch")
    gate_block = lax.dynamic_index_in_dim(gate_weight, my_block, 0, keepdims=False)
    up_block = lax.dynamic_index_in_dim(up_weight, my_block, 0, keepdims=False)
    down_block = lax.dynamic_index_in_dim(down_weight, my_block, 0, keepdims=False)
    gain_block = lax.dynamic_slice_in_dim(norm_gain, my_block * width_dev, width_dev)
    wide_mixed = to_wide(mixed_out)
    partial_sum = jnp.sum(wide_mixed * wide_mixed, axis=1)
    square_sum = lax.psum(partial_sum, "ch")
    full_width = width_dev * lax.axis_size("ch")
    inverse_rms = lax.rsqrt(square_sum / full_width + epsilon)
    normed = (wide_mixed * inverse_rms[:, None, :] * to_wide(gain_block)[:, None]).astype(
        jnp.bfloat16
    )
    gate_value = jnp.matmul(gate_block.T, normed, preferred_element_type=jnp.float32)
    up_value = jnp.matmul(up_block.T, normed, preferred_element_type=jnp.float32)
    hidden = (jax.nn.silu(gate_value) * up_value).astype(jnp.bfloat16)
    down_value = jnp.matmul(
        down_block,
        lax.all_to_all(hidden, "ch", split_axis=1, concat_axis=1, tiled=True),
        preferred_element_type=jnp.float32,
    )
    return (wide_mixed + down_value).astype(jnp.bfloat16)


def solution(mesh):
    in_specs = (
        P(None, "ch", "seq"),
        P("ch"),
        P("ch"),
        P("ch"),
        P("ch"),
        P(),
        P(None, "seq"),
        P(),
        P("ch", "seq", None),
        P(),
        P(None, "seq"),
        P(),
        P(),
        P(),
        P(),
        P(),
    )
    out_specs = P(None, "ch", "seq")
    return jax.shard_map(local, mesh=mesh, in_specs=in_specs, out_specs=out_specs, check_vma=False)
```

profile of v0, /device:TPU:1, one launch (start us, length us, event | category | flops | bytes accessed | tf_op | source)
XLA Modules:
  0.0 671.6 jit_solution(2042464481159986711)
XLA Ops:
  0.0 2.9 fusion.21
  3.7 50.5 %all_to_all.38 = bf16[1,192,8,512]{3,2,0,1:T(8,128)(2,1)S(1)} all-to-all(bf16[1,192,8,512]{3,2,0,1:T(8,128)(2,1)S(1)} %bitcast_bitcast_fusion), channel_id=1, replica_groups=mesh['seq'=64,'ch'=4] {'seq'}, dimensions={1} | all-to-all | bytes 3145728 | tf_op jit(solution)/shard_map/all_to_all | solution.py:40
  54.2 8.1 %all-to-all-start.1 = ((bf16[1,192,8,512]{3,2,0,1:T(8,128)(2,1)}), bf16[1,192,8,512]{3,2,0,1:T(8,128)(2,1)}, u32[]{:S(2)}, u32[]{:S(2)}) async-start(bf16[1,192,8,512]{3,2,0,1:T(8,128)(2,1)} %bitcast.7), calls=%async_computation.1 | async-start | bytes 3145728 | tf_op jit(solution)/shard_map/all_to_all | solution.py:41
  62.4 155.4 %all_gather.6 = bf16[512,512]{0,1:T(8,128)(2,1)S(1)} all-gather(bf16[512,8]{0,1:T(8,128)(2,1)S(1)} %copy-done.6), channel_id=1, replica_groups=mesh['seq'=64,'ch'=4] {'seq'}, dimensions={1}, use_global_device_ids=true | all-gather | bytes 532480 | tf_op jit(solution)/shard_map/all_gather | solution.py:44
  217.8 1.1 convert_element_type.89
  218.9 125.3 %all_gather.7 = bf16[512,512]{0,1:T(8,128)(2,1)S(1)} all-gather(bf16[512,8]{0,1:T(8,128)(2,1)S(1)} %copy-done.7), channel_id=1, replica_groups=mesh['seq'=64,'ch'=4] {'seq'}, dimensions={1}, use_global_device_ids=true | all-gather | bytes 532480 | tf_op jit(solution)/shard_map/all_gather | solution.py:45
  344.2 1.2 copy.46
  345.4 5.1 fusion.28
  350.5 2.5 convolution_convert_fusion.1
  354.1 3.0 copy.48
  357.1 9.5 %all-to-all-start.2 = ((bf16[1,3,512,512]{3,1,0,2:T(4,128)(2,1)}), bf16[1,3,512,512]{3,1,0,2:T(4,128)(2,1)S(1)}, u32[]{:S(2)}, u32[]{:S(2)}) async-start(bf16[1,3,512,512]{3,1,0,2:T(4,128)(2,1)} %copy.48), calls=%async_computation.2 | async-start | bytes 4194304 | tf_op jit(solution)/shard_map/all_to_all | solution.py:67
  367.4 27.7 %all-to-all-done.2 = bf16[1,3,512,512]{3,1,0,2:T(4,128)(2,1)S(1)} async-done(((bf16[1,3,512,512]{3,1,0,2:T(4,128)(2,1)}), bf16[1,3,512,512]{3,1,0,2:T(4,128)(2,1)S(1)}, u32[]{:S(2)}, u32[]{:S(2)}) %all-to-all-start.2) | async-done | bytes 1572896 | tf_op jit(solution)/shard_map/all_to_all | solution.py:67
  395.6 2.0 copy.50
  397.5 4.8 reshape.85
  402.3 4.6 fusion.13
  406.8 73.0 %psum.7 = f32[1,4096]{1,0:T(1,128)S(1)} all-reduce(f32[1,4096]{1,0:T(1,128)S(1)} %bitcast.100), channel_id=1, replica_groups=mesh['seq'=64,'ch'=4] {'ch'}, use_global_device_ids=true, to_apply=%region_1.2 | all-reduce | flops 4096 | bytes 32768 | tf_op jit(solution)/shard_map/psum | solution.py:79
  479.9 3.4 fusion.44
  483.3 4.9 fusion.3
  488.3 32.7 %copy.76 = bf16[1,768,4096]{2,0,1:T(2,128)(2,1)} copy(bf16[1,768,4096]{2,1,0:T(8,128)(2,1)S(1)} %fusion.3) | data formatting | bytes 12582912 | tf_op jit(solution)/shard_map/convert_element_type | solution.py:87
  521.4 39.9 %reduce.1 = bf16[768,4096]{1,0:T(8,128)(2,1)} reduce(bf16[768,1,4096]{2,1,0:T(2,128)(2,1)} %bitcast.95, bf16[]{:T(256)} %broadcast.25), dimensions={1}, to_apply=%bitcast.93.reduce_sub_computation | reduce | bytes 12582914
  561.4 8.1 %reshape.92 = bf16[4,2,393216]{2,1,0:T(2,128)(2,1)} reshape(bf16[768,4096]{1,0:T(8,128)(2,1)} %reduce.1) | data formatting | bytes 12582912
  569.5 78.9 %all_to_all.39 = bf16[4,2,393216]{2,1,0:T(2,128)(2,1)} all-to-all(bf16[4,2,393216]{2,1,0:T(2,128)(2,1)} %reshape.92), channel_id=1, replica_groups=mesh['seq'=64,'ch'=4] {'ch'}, dimensions={0} | all-to-all | bytes 12582912 | tf_op jit(solution)/shard_map/all_to_all | solution.py:90
  648.4 10.0 %reshape.93 = bf16[768,1,4096]{2,1,0:T(2,128)(2,1)} reshape(bf16[4,2,393216]{2,1,0:T(2,128)(2,1)} %all_to_all.39) | data formatting | bytes 12582912
  658.3 13.3 %fusion.10 = bf16[1,192,4096]{2,1,0:T(8,128)(2,1)} fusion(bf16[1,768,4096]{2,0,1:T(2,128)(2,1)} %bitcast.96, bf16[1,192,4096]{2,1,0:T(8,128)(2,1)S(1)} %copy-done.3, bf16[4,192,768]{2,1,0:T(8,128)(2,1)} %param.31, s32[]{:T(128)S(6)} %select_n.9), kind=kOutput, calls=%fused_computation.11 | convolution fusion | flops 1210318848 | bytes 16023556 | tf_op jit(solution)/shard_map/dot_general | solution.py:88
  (30 shorter events, 3.7 us)
Async XLA Ops:
  0.0 479.9 %copy-start = (bf16[4,192,768]{2,1,0:T(8,128)(2,1)S(1)}, bf16[4,192,768]{2,1,0:T(8,128)(2,1)}, u32[]{:S(2)}) copy-start(bf16[4,192,768]{2,1,0:T(8,128)(2,1)} %param.29) | copy-start | bytes 3538948
  3.7 58.7 %copy-start.6 = (bf16[512,8]{0,1:T(8,128)(2,1)S(1)}, bf16[512,8]{0,1:T(8,128)(2,1)}, u32[]{:S(2)}) copy-start(bf16[512,8]{0,1:T(8,128)(2,1)} %param.22) | copy-start | bytes 24580
  54.2 164.7 %copy-start.7 = (bf16[512,8]{0,1:T(8,128)(2,1)S(1)}, bf16[512,8]{0,1:T(8,128)(2,1)}, u32[]{:S(2)}) copy-start(bf16[512,8]{0,1:T(8,128)(2,1)} %param.26) | copy-start | bytes 24580
  54.2 291.2 %all-to-all-start.1 = ((bf16[1,192,8,512]{3,2,0,1:T(8,128)(2,1)}), bf16[1,192,8,512]{3,2,0,1:T(8,128)(2,1)}, u32[]{:S(2)}, u32[]{:S(2)}) async-start(bf16[1,192,8,512]{3,2,0,1:T(8,128)(2,1)} %bitcast.7), calls=%async_computation.1 | async-start | bytes 3145728 | tf_op jit(solution)/shard_map/all_to_all | solution.py:41
  345.4 5.1 copy-start.10
  350.5 2.6 copy-start.4
  350.5 2.6 copy-start.5
  357.1 37.9 %all-to-all-start.2 = ((bf16[1,3,512,512]{3,1,0,2:T(4,128)(2,1)}), bf16[1,3,512,512]{3,1,0,2:T(4,128)(2,1)S(1)}, u32[]{:S(2)}, u32[]{:S(2)}) async-start(bf16[1,3,512,512]{3,1,0,2:T(4,128)(2,1)} %copy.48), calls=%async_computation.2 | async-start | bytes 4194304 | tf_op jit(solution)/shard_map/all_to_all | solution.py:67
  397.5 4.8 copy-start.2
  397.5 4.8 copy-start.8
  397.5 4.8 copy-start.9
  479.9 3.4 copy-start.3
  658.3 13.3 %copy-start.1 = (bf16[4,192,768]{2,1,0:T(8,128)(2,1)S(1)}, bf16[4,192,768]{2,1,0:T(8,128)(2,1)}, u32[]{:S(2)}) copy-start(bf16[4,192,768]{2,1,0:T(8,128)(2,1)} %param.29) | copy-start | bytes 3538948
where the time goes:
time: 672 us
  blocking collectives  483 us (72%)
  local copies, waits for them, and re-layouts  62.9 us (9%)
  other arithmetic  49.8 us (7%)
  matrix products  30.3 us (5%)
  waiting for transfers between devices  27.7 us (4%)
  starting transfers between devices  17.6 us (3%)
    all_gather x1, blocking collectives, local(): lax.all_gather(twist_in, 'seq', axis=1, tiled=True)  155 us
    all_gather x1, blocking collectives, local(): lax.all_gather(twist_out, 'seq', axis=1, tiled=True)  125 us
    all_to_all x1, blocking collectives, local(): lax.all_to_all(hidden, 'ch', split_axis=1, concat_axis=1, tiled=True)  78.9 us
    psum x1, blocking collectives, local(): square_sum = lax.psum(partial_sum, 'ch')  73 us
    all_to_all x1, blocking collectives, local(): lax.all_to_all(gated_four, 'seq', split_axis=1, concat_axis=2, tiled=True)  50.5 us
    unnamed x1, other arithmetic  39.9 us
    convert_element_type x1, local copies, waits for them, and re-layouts, local(): hidden = (jax.nn.silu(gate_value) * up_value).astype(jnp.bfloat16)  32.7 us
    all_to_all x1, waiting for transfers between devices, local(): lax.all_to_all(returned, 'seq', split_axis=2, concat_axis=1, tiled=True)  27.7 us
  transfers between devices with their start and end apart: 2, of which 1 were waited for; matrix products, arithmetic and copies ran while one was open for 0% of the time, Pallas kernels for 0%

commit v1 on v0

v1 whole, which is shorter than its diff:
```python
import jax
import jax.numpy as jnp
from jax import lax
from jax.experimental import pallas as pl
from jax.experimental.pallas import tpu as pltpu
from jax.sharding import PartitionSpec as P

epsilon = 1e-05
MESH = pl.DeviceIdType.MESH
NZ, NX, NY = 8, 4, 2
NXY = NX * NY
NS = NZ * NXY
NC = 4
BF = jnp.bfloat16


def to_wide(array_in):
    return array_in.astype(jnp.float32)


def each_peer(me, core, act):
    z, x, y = lax.div(me, NXY), lax.rem(lax.div(me, NY), NX), lax.rem(me, NY)
    layers = [lax.rem(z + (3 + 2 * core) * low, NZ) * NXY for low in range(NZ)]

    def peer(high, low):
        new_x = lax.rem(x + (high + low) * (1 + 2 * core), NX)
        new_y = lax.rem(y + lax.div(high, NX) + low // NX, NY)
        return layers[low] + new_x * NY + new_y

    for low in range(1, NZ):
        act(peer(jnp.int32(0), low))

    def row(high, carry):
        for low in range(NZ):
            act(peer(high, low))
        return carry

    lax.fori_loop(1, NXY, row, 0)


def turned_dot(left, right):
    return lax.dot_general(left, right, (((1,), (1,)), ((), ())), preferred_element_type=jnp.float32)


def dot(left, right):
    return jnp.dot(left, right, preferred_element_type=jnp.float32)


def layer_kernel(
    slope_in,
    shift_in,
    slope_out,
    shift_out,
    gain_ref,
    twist_in_ref,
    twist_out_ref,
    stream_any,
    kernel_any,
    first_any,
    second_any,
    third_any,
    fourth_any,
    gate_any,
    up_any,
    down_any,
    out_ref,
    stream_ref,
    kernel_ref,
    mixes,
    gate_ref,
    up_ref,
    down_ref,
    param_ref,
    gains,
    twist_ref,
    gated,
    send,
    got,
    tables,
    table_in,
    table_out,
    held,
    back,
    home,
    wide_home,
    half,
    own_gate,
    mixed,
    turned,
    chosen,
    normed,
    hidden,
    leaving,
    load_sem,
    send_sem,
    got_sem,
    twist_sem,
    home_sem,
    half_sem,
    swap_sem,
    out_sem,
    plane_sem,
    side_sem,
):
    me = lax.axis_index("seq")
    ch = lax.axis_index("ch")
    core = lax.rem(ch, 2)
    side = lax.div(ch, 2)
    across = (1 - side) * 2 + core
    partner = side * 2 + 1 - core
    my_z, my_xy = lax.div(me, NXY), lax.rem(me, NXY)
    few = got.shape[0]

    loads = [
        pltpu.make_async_copy(source, target, load_sem.at[i])
        for i, (source, target) in enumerate(
            (
                (stream_any, stream_ref),
                (kernel_any, kernel_ref),
                (first_any, mixes.at[0]),
                (second_any, mixes.at[1]),
                (third_any, mixes.at[2]),
                (fourth_any, mixes.at[3]),
                (gate_any, gate_ref),
                (up_any, up_ref),
                (down_any, down_ref),
            )
        )
    ]
    for load in loads:
        load.start()

    barrier = pltpu.get_barrier_semaphore()

    columns = [lax.rem(my_z + 3 * q, NZ) * NXY + my_xy for q in range(1, NZ)]
    planes = [my_z * NXY + lax.rem(my_xy + q, NXY) for q in range(1, NXY)]
    for peer in columns + planes:
        pl.semaphore_signal(barrier, 1, device_id={"seq": peer}, device_id_type=MESH)
    for q in range(1, NC):
        pl.semaphore_signal(barrier, 1, device_id={"ch": lax.rem(ch + q, NC)}, device_id_type=MESH)

    def spread(row):
        return jnp.broadcast_to(row, (128, row.shape[1])).T

    for i, row in enumerate((slope_in, shift_in, slope_out, shift_out)):
        param_ref[i] = spread(row[...])
    twist_ref[...] = jnp.concatenate(
        [to_wide(twist_in_ref[...]), to_wide(twist_out_ref[...])], axis=0
    ).astype(BF)

    def pack(c):
        rows = slice(64 * c, 64 * c + 64)
        slope, shift = param_ref[0, rows, :], param_ref[1, rows, :]

        def one(i, carry):
            for q in range(4):
                lanes = pl.ds(pl.multiple_of(i * 512 + q * 128, 128), 128)
                value = to_wide(stream_ref[rows, lanes])
                value = value * jax.nn.sigmoid(value * slope + shift)
                gated[q, pl.ds(i, 64, stride=8), :] = value
            return carry

        lax.fori_loop(0, 8, one, 0)
        for q in range(4):
            lanes = slice(128 * q, 128 * q + 128)
            top = gated[q].reshape(64, 8, 128)
            low = to_wide(kernel_ref[rows, :, lanes])
            send[c, :, :, lanes] = jnp.concatenate([top, low], axis=1).astype(BF)

    def send_lines(c):
        def one(peer):
            pltpu.make_async_remote_copy(
                src_ref=send.at[c, peer],
                dst_ref=got.at[c, me],
                send_sem=send_sem.at[1],
                recv_sem=got_sem.at[c],
                device_id={"seq": peer},
                device_id_type=MESH,
            ).start()

        each_peer(me, core, one)
        got[c, me] = send[c, me]

    def bytes_of(ref, sem):
        pltpu.make_async_copy(ref, ref, sem).wait()

    loads[0].wait()
    loads[1].wait()
    pack(0)
    pl.semaphore_wait(barrier, NZ - 1 + NXY - 1 + NC - 1)
    for peer in planes:
        pl.semaphore_signal(plane_sem, 1, device_id={"seq": peer}, device_id_type=MESH)

    lanes = pl.ds(pl.multiple_of(ch * 128, 128), 128)
    for peer in columns:
        pltpu.make_async_remote_copy(
            src_ref=twist_ref.at[:, lanes],
            dst_ref=tables.at[ch, my_xy, my_z],
            send_sem=send_sem.at[0],
            recv_sem=twist_sem.at[0],
            device_id={"seq": peer},
            device_id_type=MESH,
        ).start()
    tables[ch, my_xy, my_z] = twist_ref[:, lanes]
    pl.semaphore_wait(plane_sem, NXY - 1)
    pl.semaphore_signal(side_sem, 1, device_id={"ch": across}, device_id_type=MESH)
    send_lines(0)
    pack(1)
    send_lines(1)
    bytes_of(tables.at[0, 0, pl.ds(0, NZ - 1)], twist_sem.at[0])
    for peer in planes:
        pltpu.make_async_remote_copy(
            src_ref=tables.at[ch, my_xy],
            dst_ref=tables.at[ch, my_xy],
            send_sem=send_sem.at[4],
            recv_sem=twist_sem.at[1],
            device_id={"seq": peer},
            device_id_type=MESH,
        ).start()
    pack(2)
    send_lines(2)
    bytes_of(tables.at[0, pl.ds(0, NXY - 1)], twist_sem.at[1])
    for q in range(1, NC):
        pltpu.make_async_remote_copy(
            src_ref=tables.at[ch],
            dst_ref=tables.at[ch],
            send_sem=send_sem.at[5],
            recv_sem=twist_sem.at[2],
            device_id={"ch": lax.rem(ch + q, NC)},
            device_id_type=MESH,
        ).start()
    for i in range(8):
        for e in range(2):
            lanes = pl.ds(pl.multiple_of(i * 512 + 256 * (1 - side) + 128 * e, 128), 128)
            pltpu.make_async_remote_copy(
                src_ref=stream_ref.at[:, lanes],
                dst_ref=half.at[side, :, pl.ds(e * 1024 + i * 128, 128)],
                send_sem=send_sem.at[2],
                recv_sem=half_sem.at[0],
                device_id={"ch": across},
                device_id_type=MESH,
            ).start()
    pltpu.make_async_remote_copy(
        src_ref=param_ref.at[pl.ds(2, 2)],
        dst_ref=own_gate.at[side],
        send_sem=send_sem.at[3],
        recv_sem=half_sem.at[1],
        device_id={"ch": across},
        device_id_type=MESH,
    ).start()

    for i in range(8):
        for e in range(2):
            lanes = pl.ds(pl.multiple_of(i * 512 + 256 * side + 128 * e, 128), 128)
            half[side, :, e * 1024 + i * 128 : e * 1024 + i * 128 + 128] = stream_ref[:, lanes]
    own_gate[side] = param_ref[2:4]
    gains[...] = spread(to_wide(gain_ref[...]).reshape(1, 768))

    for load in loads[2:]:
        load.wait()

    def choose(n, carry):
        for w, source in enumerate((gate_ref, up_ref)):
            turned[...] = to_wide(source[n]).T.astype(BF)
            for j, k in enumerate((ch, across)):
                chosen[n, (2 * j + w) * 192 : (2 * j + w + 1) * 192, :] = turned[
                    pl.ds(pl.multiple_of(k * 192, 192), 192), :
                ]
        return carry

    lax.fori_loop(0, NC, choose, 0)

    bytes_of(tables.at[pl.ds(0, NC - 1)], twist_sem.at[2])
    for q in range(NC):
        rows = slice(q * 128, (q + 1) * 128)
        part = to_wide(tables[q])
        part = jnp.concatenate([part[:, z] for z in range(NZ)], axis=0)
        part = part.reshape(NS, 2, 8, 128)
        table_in[rows, :] = part[:, 0].reshape(NS * 8, 128).T
        table_out[rows, :] = part[:, 1].reshape(NS * 8, 128).T

    def arrive(c):
        bytes_of(got.at[c, pl.ds(0, NS - 1)], got_sem.at[c])

    def mix(c):
        block = to_wide(got[c]).reshape(NS, 2, 8, 512)
        lines = block[:, 0].reshape(512, 512).astype(BF)
        value = dot(mixes[0], lines)
        value = (value * table_in[...]).astype(BF)
        value = turned_dot(value, mixes[1])
        block = to_wide(got[c]).reshape(NS, 2, 8, 512)
        value = (value * block[:, 1].reshape(512, 512)).astype(BF)
        value = turned_dot(value, mixes[2])
        value = (to_wide(value.astype(BF)) * table_out[...]).astype(BF)
        return dot(mixes[3], value)

    def quarter(value, h, e):
        start = 256 * h + 128 * e
        return value[:, start : start + 128].reshape(NS, 8, 128)

    def send_back(step, same=True, far=True):
        def one(peer, near):
            to_side, to_ch = (side, ch) if near else (1 - side, across)
            pltpu.make_async_remote_copy(
                src_ref=back.at[step, to_side, peer],
                dst_ref=home.at[step, side, me],
                send_sem=send_sem.at[6],
                recv_sem=home_sem.at[step, 0 if near else 1],
                device_id={"seq": peer, "ch": to_ch},
                device_id_type=MESH,
            ).start()

        def both(peer):
            if same:
                one(peer, True)
            if far:
                one(peer, False)

        each_peer(me, core, both)
        if far:
            one(me, False)
        if same:
            home[step, side, me] = back[step, side, me]

    def widen(step):
        bytes_of(home.at[step, 0, pl.ds(0, NS - 1)], home_sem.at[step, 0])
        bytes_of(home.at[step, 0], home_sem.at[step, 1])
        for y in range(2):
            wide_home[step, y] = to_wide(home[step, y]).reshape(NS * 16, 128)

    def gate_out(c, e, i):
        step, row = (0, e * 8 + i) if c == 0 else (1 + e, (c - 1) * 8 + i)
        rows = slice(64 * c, 64 * c + 64)
        lanes = slice(e * 1024 + i * 128, e * 1024 + i * 128 + 128)

        def one(y, carry):
            slope, shift = own_gate[y, 0, rows, :], own_gate[y, 1, rows, :]
            value = to_wide(half[y, rows, lanes])
            came = wide_home[step, y, pl.ds(row, 64, stride=16), :]
            value = value + came * jax.nn.sigmoid(value * slope + shift)
            mixed[core, y, rows, lanes] = value.astype(BF)
            return carry

        lax.fori_loop(0, 2, one, 0)

    def swap(rows, tokens, sem):
        part = mixed.at[core, :, rows, tokens]
        pltpu.make_async_remote_copy(
            src_ref=part,
            dst_ref=part,
            send_sem=send_sem.at[8],
            recv_sem=sem,
            device_id={"ch": partner},
            device_id_type=MESH,
        ).start()

    arrive(0)
    value = mix(0)
    for h in range(2):
        back[0, h] = jnp.concatenate([quarter(value, h, 0), quarter(value, h, 1)], axis=1).astype(
            BF
        )
    arrive(1)
    held[...] = mix(1)
    pl.semaphore_wait(side_sem, 1)
    send_back(0, same=False)
    arrive(2)
    send_back(0, far=False)
    value = mix(2)
    for e in range(2):
        for h in range(2):
            back[1 + e, h] = jnp.concatenate(
                [quarter(held, h, e), quarter(value, h, e)], axis=1
            ).astype(BF)
    send_back(1)
    bytes_of(half.at[0], half_sem.at[0])
    bytes_of(own_gate.at[0], half_sem.at[1])
    widen(0)
    for e in range(2):
        for i in range(8):
            gate_out(0, e, i)
    swap(pl.ds(0, 64), pl.ds(0, 2048), swap_sem.at[0])
    send_back(2)

    def normalize(start, size):
        tokens = slice(start, start + size)
        slot = tokens
        total = jnp.zeros((1, size), jnp.float32)
        for n in range(NC):
            value = to_wide(mixed[n % 2, n // 2, :, tokens])
            total = total + jnp.sum(value * value, axis=0, keepdims=True)
        inverse = lax.rsqrt(total / 768.0 + epsilon)
        for n in range(NC):
            value = to_wide(mixed[n % 2, n // 2, :, tokens])
            gain = gains[192 * n : 192 * n + 192, :]
            gain = jnp.concatenate([gain] * (size // 128), axis=1)
            normed[192 * n : 192 * n + 192, slot] = (value * inverse * gain).astype(BF)

    def block(start, size, j):
        tokens = slice(start, start + size)
        slot = tokens
        for n in range(NC):
            wide = dot(
                chosen[n, 384 * j : 384 * j + 384, :], normed[192 * n : 192 * n + 192, slot]
            )
            gate, up = wide[:192], wide[192:]
            hidden[192 * n : 192 * n + 192, :size] = (gate / (1.0 + jnp.exp(-gate)) * up).astype(BF)
        value = dot(down_ref[(ch, across)[j]], hidden[:, :size])
        return (to_wide(mixed[core, (side, 1 - side)[j], :, tokens]) + value).astype(BF)

    def place(token):
        start = 512 * (token % 1024 // 128) + 256 * side + 128 * (token // 1024)
        return pl.ds(pl.multiple_of(start, 128), 128)

    def across_block(start, size):
        leaving[:, start : start + size] = block(start, size, 1)
        for token in range(start, start + size, 128):
            pltpu.make_async_remote_copy(
                src_ref=leaving.at[:, pl.ds(token, 128)],
                dst_ref=out_ref.at[:, place(token)],
                send_sem=send_sem.at[9],
                recv_sem=out_sem,
                device_id={"ch": across},
                device_id_type=MESH,
            ).start()

    def own_block(start, size):
        value = block(start, size, 0)
        for i in range(0, size, 128):
            out_ref[:, place(start + i)] = value[:, i : i + 128]

    for e, size, first in ((0, 512, 1), (1, 256, 3)):
        widen(1 + e)
        starts = range(1024 * e, 1024 * e + 1024, size)
        for t, start in enumerate(starts):
            for i in range(start % 1024 // 128, (start % 1024 + size) // 128):
                gate_out(1, e, i)
                gate_out(2, e, i)
            swap(pl.ds(64, 128), pl.ds(start, size), swap_sem.at[first + t])
        if e == 0:
            bytes_of(mixed.at[0, :, pl.ds(0, 64)], swap_sem.at[0])
        for t, start in enumerate(starts):
            bytes_of(mixed.at[0, :, pl.ds(64, 128), pl.ds(start, size)], swap_sem.at[first + t])
            normalize(start, size)
            across_block(start, size)

    for start in range(0, 2048, 512):
        own_block(start, 512)

    bytes_of(leaving, out_sem)
    bytes_of(leaving, send_sem.at[9])
    bytes_of(mixed.at[0], send_sem.at[8])
    for step in range(3):
        bytes_of(home.at[step, 0, pl.ds(0, NS - 1)], send_sem.at[6])
        bytes_of(home.at[step, 0], send_sem.at[6])
    for c in range(few):
        bytes_of(got.at[c, pl.ds(0, NS - 1)], send_sem.at[1])
    bytes_of(tables.at[0, 0, pl.ds(0, NZ - 1)], send_sem.at[0])
    bytes_of(tables.at[0, pl.ds(0, NXY - 1)], send_sem.at[4])
    bytes_of(tables.at[pl.ds(0, NC - 1)], send_sem.at[5])
    bytes_of(half.at[0], send_sem.at[2])
    bytes_of(own_gate.at[0], send_sem.at[3])


def local(
    stream,
    in_weight,
    in_bias,
    out_weight,
    out_bias,
    first_mix,
    twist_in,
    second_mix,
    kernel,
    third_mix,
    twist_out,
    fourth_mix,
    norm_gain,
    gate_weight,
    up_weight,
    down_weight,
):
    _, width, tokens = stream.shape
    few = width // NS
    fast = pl.BlockSpec(memory_space=pltpu.VMEM)
    slow = pl.BlockSpec(memory_space=pl.ANY)
    wide, half = jnp.float32, BF
    dma = pltpu.SemaphoreType.DMA
    out = pl.pallas_call(
        layer_kernel,
        out_shape=pltpu.VMEM((width, tokens), BF),
        in_specs=[fast] * 7 + [slow] * 9,
        out_specs=fast,
        scratch_shapes=[
            pltpu.VMEM((width, tokens), half),
            pltpu.VMEM(kernel.shape, half),
            pltpu.VMEM((4, 512, 512), half),
            pltpu.VMEM(gate_weight.shape, half),
            pltpu.VMEM(up_weight.shape, half),
            pltpu.VMEM(down_weight.shape, half),
            pltpu.VMEM((4, width, 128), wide),
            pltpu.VMEM((4 * width, 128), wide),
            pltpu.VMEM((16, 512), half),
            pltpu.VMEM((4, 512, 128), wide),
            pltpu.VMEM((few, NS, 16, 512), half),
            pltpu.VMEM((few, NS, 16, 512), half),
            pltpu.VMEM((NC, NXY, NZ, 16, 128), half),
            pltpu.VMEM((512, 512), wide),
            pltpu.VMEM((512, 512), wide),
            pltpu.VMEM((512, 512), wide),
            pltpu.VMEM((3, 2, NS, 16, 128), half),
            pltpu.VMEM((3, 2, NS, 16, 128), half),
            pltpu.VMEM((3, 2, NS * 16, 128), wide),
            pltpu.VMEM((2, width, tokens // 2), half),
            pltpu.VMEM((2, 2, width, 128), wide),
            pltpu.VMEM((2, 2, width, tokens // 2), half),
            pltpu.VMEM((4 * width, width), half),
            pltpu.VMEM((NC, 4 * width, width), half),
            pltpu.VMEM((4 * width, tokens // 2), half),
            pltpu.VMEM((4 * width, 512), half),
            pltpu.VMEM((width, tokens // 2), half),
            dma((9,)),
            dma((10,)),
            dma((few,)),
            dma((3,)),
            dma((3, 2)),
            dma((2,)),
            dma((7,)),
            dma,
            pltpu.SemaphoreType.REGULAR,
            pltpu.SemaphoreType.REGULAR,
        ],
        compiler_params=pltpu.CompilerParams(
            collective_id=0, has_side_effects=True, vmem_limit_bytes=58 * 2**20
        ),
    )(
        in_weight.reshape(1, width),
        in_bias.reshape(1, width),
        out_weight.reshape(1, width),
        out_bias.reshape(1, width),
        norm_gain,
        twist_in.T,
        twist_out.T,
        stream[0],
        kernel,
        first_mix,
        second_mix,
        third_mix,
        fourth_mix,
        gate_weight,
        up_weight,
        down_weight,
    )
    return out[None]


def solution(mesh):
    in_specs = (
        P(None, "ch", "seq"),
        P("ch"),
        P("ch"),
        P("ch"),
        P("ch"),
        P(),
        P(None, "seq"),
        P(),
        P("ch", "seq", None),
        P(),
        P(None, "seq"),
        P(),
        P(),
        P(),
        P(),
        P(),
    )
    out_specs = P(None, "ch", "seq")
    return jax.shard_map(local, mesh=mesh, in_specs=in_specs, out_specs=out_specs, check_vma=False)
```

time: 672 us -> 134 us (0.20)
  blocking collectives: 483 us -> 0 us
  Pallas kernels: 0 us -> 133 us
  local copies, waits for them, and re-layouts: 62.9 us -> 1.15 us
  other arithmetic: 49.8 us -> 0 us
  matrix products: 30.3 us -> 0 us
  waiting for transfers between devices: 27.7 us -> 0 us
  starting transfers between devices: 17.6 us -> 0 us
    all_gather x2 -> x0, blocking collectives: 281 us -> none  [the longest x1 155 us: local(): lax.all_gather(twist_in, 'seq', axis=1, tiled=True)]
    pallas_call x0 -> x1, Pallas kernels: none -> 133 us  [local(): pl.pallas_call(layer_kernel, out_shape=pltpu.VMEM((width, tokens), BF), i...]
    all_to_all x2 -> x0, blocking collectives: 129 us -> none  [the longest x1 78.9 us: local(): lax.all_to_all(hidden, 'ch', split_axis=1, concat_axis=1, tiled=True)]
    psum x1 -> x0, blocking collectives: 73 us -> none  [local(): square_sum = lax.psum(partial_sum, 'ch')]
    convert_element_type x4 -> x0, local copies, waits for them, and re-layouts: 40.5 us -> none  [the longest x1 32.7 us: local(): hidden = (jax.nn.silu(gate_value) * up_value).astype(jnp.bfloat16)]
    unnamed x1 -> x0, other arithmetic: 39.9 us -> none
    dot_general x6 -> x0, matrix products: 30.3 us -> none  [the longest x1 13.3 us: local(): jnp.matmul(down_block, lax.all_to_all(hidden, 'ch', split_axis=1, concat_...]
    all_to_all x2 -> x0, waiting for transfers between devices: 27.7 us -> none  [the longest x1 27.7 us: local(): lax.all_to_all(returned, 'seq', split_axis=2, concat_axis=1, tiled=True)]
  transfers between devices with their start and end apart: 2 -> 0, of which waited for: 1 -> 0; matrix products, arithmetic and copies ran while one was open for 0% -> 0% of each run, Pallas kernels for 0% -> 0%
where the time goes in v1:
time: 134 us
  Pallas kernels  133 us (99%)
    pallas_call x1, Pallas kernels, local(): pl.pallas_call(layer_kernel, out_shape=pltpu.VMEM((width, tokens), BF), i...  133 us

profile of v1, /device:TPU:1, one launch (start us, length us, event | category | flops | bytes accessed | tf_op | source)
XLA Modules:
  0.0 134.1 jit_solution(6024168875576965664)
XLA Ops:
  0.0 133.0 %shard_map.154 = bf16[192,4096]{1,0:T(8,128)(2,1)S(1)} custom-call(f32[1,192]{1,0:T(1,128)} %bitcast.12, f32[1,192]{1,0:T(1,128)} %bitcast.13, f32[1,192]{1,0:T(1,128)} %bitcast.14, f32[1,192]{1,0:T(1,128)} %bitcast.15, bf16[768]{0:T(1024)(128)(2,1)} %gain_ref.1, bf16[8,512]{1,0:T(8,128)(2,1)} %bitcast.10, bf16[8,512]{1,0:T(8,128)(2,1)} %bitcast.11, ...), custom_call_target="tpu_custom_call" | custom-call | tf_op jit(solution)/shard_map/pallas_call | solution.py:489
  133.0 1.1 copy.18

commit v2 on v1

--- a/solution.py
+++ b/solution.py
@@ -36,6 +36,11 @@
         return carry
 
     lax.fori_loop(1, NXY, row, 0)
+
+
+def gate_by(value, score):
+    value = 0.5 * value
+    return value + value * jnp.tanh(0.5 * score)
 
 
 def turned_dot(left, right):
@@ -156,7 +161,7 @@
             for q in range(4):
                 lanes = pl.ds(pl.multiple_of(i * 512 + q * 128, 128), 128)
                 value = to_wide(stream_ref[rows, lanes])
-                value = value * jax.nn.sigmoid(value * slope + shift)
+                value = gate_by(value, value * slope + shift)
                 gated[q, pl.ds(i, 64, stride=8), :] = value
             return carry
 
@@ -298,6 +303,16 @@
         start = 256 * h + 128 * e
         return value[:, start : start + 128].reshape(NS, 8, 128)
 
+    def far_copy(step, peer):
+        return pltpu.make_async_remote_copy(
+            src_ref=back.at[step, 1 - side, peer],
+            dst_ref=home.at[step, side, me],
+            send_sem=send_sem.at[6],
+            recv_sem=home_sem.at[step, 1],
+            device_id={"seq": peer, "ch": across},
+            device_id_type=MESH,
+        )
+
     def send_back(step, same=True, far=True):
         def one(peer, near):
             to_side, to_ch = (side, ch) if near else (1 - side, across)
@@ -318,9 +333,23 @@
 
         each_peer(me, core, both)
         if far:
-            one(me, False)
+            far_copy(step, me).start()
         if same:
             home[step, side, me] = back[step, side, me]
+
+    def send_last(late):
+        def one(peer):
+            to_side = lax.rem(lax.div(peer, NXY) + lax.div(peer, NY) + peer + late, 2)
+            pltpu.make_async_remote_copy(
+                src_ref=back.at[2, to_side, peer],
+                dst_ref=home.at[2, side, me],
+                send_sem=send_sem.at[6],
+                recv_sem=home_sem.at[2, lax.rem(to_side + side, 2)],
+                device_id={"seq": peer, "ch": to_side * 2 + core},
+                device_id_type=MESH,
+            ).start()
+
+        each_peer(me, core, one)
 
     def widen(step):
         bytes_of(home.at[step, 0, pl.ds(0, NS - 1)], home_sem.at[step, 0])
@@ -337,7 +366,7 @@
             slope, shift = own_gate[y, 0, rows, :], own_gate[y, 1, rows, :]
             value = to_wide(half[y, rows, lanes])
             came = wide_home[step, y, pl.ds(row, 64, stride=16), :]
-            value = value + came * jax.nn.sigmoid(value * slope + shift)
+            value = value + gate_by(came, value * slope + shift)
             mixed[core, y, rows, lanes] = value.astype(BF)
             return carry
 
@@ -380,7 +409,10 @@
         for i in range(8):
             gate_out(0, e, i)
     swap(pl.ds(0, 64), pl.ds(0, 2048), swap_sem.at[0])
-    send_back(2)
+    send_last(0)
+    far_copy(2, me).start()
+    send_last(1)
+    home[2, side, me] = back[2, side, me]
 
     def normalize(start, size):
         tokens = slice(start, start + size)
@@ -404,7 +436,7 @@
                 chosen[n, 384 * j : 384 * j + 384, :], normed[192 * n : 192 * n + 192, slot]
             )
             gate, up = wide[:192], wide[192:]
-            hidden[192 * n : 192 * n + 192, :size] = (gate / (1.0 + jnp.exp(-gate)) * up).astype(BF)
+            hidden[192 * n : 192 * n + 192, :size] = (gate_by(gate, gate) * up).astype(BF)
         value = dot(down_ref[(ch, across)[j]], hidden[:, :size])
         return (to_wide(mixed[core, (side, 1 - side)[j], :, tokens]) + value).astype(BF)
 
@@ -439,12 +471,14 @@
             swap(pl.ds(64, 128), pl.ds(start, size), swap_sem.at[first + t])
         if e == 0:
             bytes_of(mixed.at[0, :, pl.ds(0, 64)], swap_sem.at[0])
+        if e == 1:
+            own_block(0, 512)
         for t, start in enumerate(starts):
             bytes_of(mixed.at[0, :, pl.ds(64, 128), pl.ds(start, size)], swap_sem.at[first + t])
             normalize(start, size)
             across_block(start, size)
 
-    for start in range(0, 2048, 512):
+    for start in range(512, 2048, 512):
         own_block(start, 512)
 
     bytes_of(leaving, out_sem)

time: 134 us -> 134 us (level)
  no operation moved by 1% of the time
where the time goes in v2:
time: 134 us; the launch traced here: 133 us
  Pallas kernels  132 us (99%)
    pallas_call x1, Pallas kernels, local(): pl.pallas_call(layer_kernel, out_shape=pltpu.VMEM((width, tokens), BF), i...  132 us

profile of v2, /device:TPU:1, one launch (start us, length us, event | category | flops | bytes accessed | tf_op | source)
XLA Modules:
  0.0 133.5 jit_solution(2318344452098803359)
XLA Ops:
  0.0 132.3 %shard_map.154 = bf16[192,4096]{1,0:T(8,128)(2,1)S(1)} custom-call(f32[1,192]{1,0:T(1,128)} %bitcast.12, f32[1,192]{1,0:T(1,128)} %bitcast.13, f32[1,192]{1,0:T(1,128)} %bitcast.14, f32[1,192]{1,0:T(1,128)} %bitcast.15, bf16[768]{0:T(1024)(128)(2,1)} %gain_ref.1, bf16[8,512]{1,0:T(8,128)(2,1)} %bitcast.10, bf16[8,512]{1,0:T(8,128)(2,1)} %bitcast.11, ...), custom_call_target="tpu_custom_call" | custom-call | tf_op jit(solution)/shard_map/pallas_call | solution.py:523
  132.3 1.1 copy.18

commit v3 on v1

--- a/solution.py
+++ b/solution.py
@@ -36,6 +36,26 @@
         return carry
 
     lax.fori_loop(1, NXY, row, 0)
+
+
+ROWS = {}
+for _step, _parts in enumerate(
+    (
+        ((0, 0, 10), (1, 0, 6)),
+        ((1, 6, 10), (2, 0, 10), (0, 10, 12)),
+        ((0, 12, 16), (1, 10, 16), (2, 10, 16)),
+    )
+):
+    _spot = 0
+    for _c, _low, _high in _parts:
+        for _row in range(_low, _high):
+            ROWS[_c, _row] = (_step, _spot)
+            _spot += 1
+
+
+def gate_by(value, score):
+    value = 0.5 * value
+    return value + value * jnp.tanh(0.5 * score)
 
 
 def turned_dot(left, right):
@@ -80,6 +100,7 @@
     table_in,
     table_out,
     held,
+    wide_back,
     back,
     home,
     wide_home,
@@ -156,7 +177,7 @@
             for q in range(4):
                 lanes = pl.ds(pl.multiple_of(i * 512 + q * 128, 128), 128)
                 value = to_wide(stream_ref[rows, lanes])
-                value = value * jax.nn.sigmoid(value * slope + shift)
+                value = gate_by(value, value * slope + shift)
                 gated[q, pl.ds(i, 64, stride=8), :] = value
             return carry
 
@@ -294,9 +315,20 @@
         value = (to_wide(value.astype(BF)) * table_out[...]).astype(BF)
         return dot(mixes[3], value)
 
-    def quarter(value, h, e):
-        start = 256 * h + 128 * e
-        return value[:, start : start + 128].reshape(NS, 8, 128)
+    def spread_rows(c):
+        value = mix(c)
+        for q in range(4):
+            held[q] = value[:, 128 * q : 128 * q + 128]
+        for h in range(2):
+            for row in range(16):
+                step, spot = ROWS[c, row]
+                wide_back[step, h, pl.ds(spot, NS, stride=16), :] = held[
+                    2 * h + row // 8, pl.ds(row % 8, NS, stride=8), :
+                ]
+
+    def finish(step):
+        for h in range(2):
+            back[step, h] = wide_back[step, h].reshape(NS, 16, 128).astype(BF)
 
     def send_back(step, same=True, far=True):
         def one(peer, near):
@@ -328,23 +360,28 @@
         for y in range(2):
             wide_home[step, y] = to_wide(home[step, y]).reshape(NS * 16, 128)
 
-    def gate_out(c, e, i):
-        step, row = (0, e * 8 + i) if c == 0 else (1 + e, (c - 1) * 8 + i)
+    def gate_out(c, token_row):
+        step, spot = ROWS[c, token_row]
         rows = slice(64 * c, 64 * c + 64)
-        lanes = slice(e * 1024 + i * 128, e * 1024 + i * 128 + 128)
+        lanes = slice(token_row * 128, token_row * 128 + 128)
 
         def one(y, carry):
             slope, shift = own_gate[y, 0, rows, :], own_gate[y, 1, rows, :]
             value = to_wide(half[y, rows, lanes])
-            came = wide_home[step, y, pl.ds(row, 64, stride=16), :]
-            value = value + came * jax.nn.sigmoid(value * slope + shift)
+            came = wide_home[step, y, pl.ds(spot, 64, stride=16), :]
+            value = value + gate_by(came, value * slope + shift)
             mixed[core, y, rows, lanes] = value.astype(BF)
             return carry
 
         lax.fori_loop(0, 2, one, 0)
 
-    def swap(rows, tokens, sem):
-        part = mixed.at[core, :, rows, tokens]
+    def gate_step(step, low, high):
+        for (c, token_row), (where, _) in ROWS.items():
+            if where == step and low <= token_row < high:
+                gate_out(c, token_row)
+
+    def swap(tokens, sem):
+        part = mixed.at[core, :, :, tokens]
         pltpu.make_async_remote_copy(
             src_ref=part,
             dst_ref=part,
@@ -355,31 +392,22 @@
         ).start()
 
     arrive(0)
-    value = mix(0)
-    for h in range(2):
-        back[0, h] = jnp.concatenate([quarter(value, h, 0), quarter(value, h, 1)], axis=1).astype(
-            BF
-        )
+    spread_rows(0)
     arrive(1)
-    held[...] = mix(1)
+    spread_rows(1)
+    finish(0)
     pl.semaphore_wait(side_sem, 1)
     send_back(0, same=False)
     arrive(2)
     send_back(0, far=False)
-    value = mix(2)
-    for e in range(2):
-        for h in range(2):
-            back[1 + e, h] = jnp.concatenate(
-                [quarter(held, h, e), quarter(value, h, e)], axis=1
-            ).astype(BF)
+    spread_rows(2)
+    finish(1)
     send_back(1)
+    finish(2)
     bytes_of(half.at[0], half_sem.at[0])
     bytes_of(own_gate.at[0], half_sem.at[1])
     widen(0)
-    for e in range(2):
-        for i in range(8):
-            gate_out(0, e, i)
-    swap(pl.ds(0, 64), pl.ds(0, 2048), swap_sem.at[0])
+    gate_step(0, 0, 16)
     send_back(2)
 
     def normalize(start, size):
@@ -404,7 +432,7 @@
                 chosen[n, 384 * j : 384 * j + 384, :], normed[192 * n : 192 * n + 192, slot]
             )
             gate, up = wide[:192], wide[192:]
-            hidden[192 * n : 192 * n + 192, :size] = (gate / (1.0 + jnp.exp(-gate)) * up).astype(BF)
+            hidden[192 * n : 192 * n + 192, :size] = (gate_by(gate, gate) * up).astype(BF)
         value = dot(down_ref[(ch, across)[j]], hidden[:, :size])
         return (to_wide(mixed[core, (side, 1 - side)[j], :, tokens]) + value).astype(BF)
 
@@ -429,22 +457,24 @@
         for i in range(0, size, 128):
             out_ref[:, place(start + i)] = value[:, i : i + 128]
 
-    for e, size, first in ((0, 512, 1), (1, 256, 3)):
+    chunks = ((0, 512), (512, 512), (1024, 256), (1280, 256), (1536, 256), (1792, 256))
+    for e, low, high in ((0, 0, 3), (1, 3, 6)):
         widen(1 + e)
-        starts = range(1024 * e, 1024 * e + 1024, size)
-        for t, start in enumerate(starts):
-            for i in range(start % 1024 // 128, (start % 1024 + size) // 128):
-                gate_out(1, e, i)
-                gate_out(2, e, i)
-            swap(pl.ds(64, 128), pl.ds(start, size), swap_sem.at[first + t])
-        if e == 0:
-            bytes_of(mixed.at[0, :, pl.ds(0, 64)], swap_sem.at[0])
-        for t, start in enumerate(starts):
-            bytes_of(mixed.at[0, :, pl.ds(64, 128), pl.ds(start, size)], swap_sem.at[first + t])
+        for t in range(low, high):
+            start, size = chunks[t]
+            for step in range(e, 2 + e):
+                if step > 0:
+                    gate_step(step, start // 128, (start + size) // 128)
+            swap(pl.ds(start, size), swap_sem.at[t])
+        if e == 1:
+            own_block(0, 512)
+        for t in range(low, high):
+            start, size = chunks[t]
+            bytes_of(mixed.at[0, :, :, pl.ds(start, size)], swap_sem.at[t])
             normalize(start, size)
             across_block(start, size)
 
-    for start in range(0, 2048, 512):
+    for start in range(512, 2048, 512):
         own_block(start, 512)
 
     bytes_of(leaving, out_sem)
@@ -507,7 +537,8 @@
             pltpu.VMEM((NC, NXY, NZ, 16, 128), half),
             pltpu.VMEM((512, 512), wide),
             pltpu.VMEM((512, 512), wide),
-            pltpu.VMEM((512, 512), wide),
+            pltpu.VMEM((4, 512, 128), wide),
+            pltpu.VMEM((3, 2, NS * 16, 128), wide),
             pltpu.VMEM((3, 2, NS, 16, 128), half),
             pltpu.VMEM((3, 2, NS, 16, 128), half),
             pltpu.VMEM((3, 2, NS * 16, 128), wide),

time: 134 us -> 134 us (level)
  no operation moved by 1% of the time
where the time goes in v3:
time: 134 us
  Pallas kernels  133 us (99%)
    pallas_call x1, Pallas kernels, local(): pl.pallas_call(layer_kernel, out_shape=pltpu.VMEM((width, tokens), BF), i...  133 us

profile of v3, /device:TPU:1, one launch (start us, length us, event | category | flops | bytes accessed | tf_op | source)
XLA Modules:
  0.0 134.0 jit_solution(993770793423394165)
XLA Ops:
  0.0 132.9 %shard_map.154 = bf16[192,4096]{1,0:T(8,128)(2,1)S(1)} custom-call(f32[1,192]{1,0:T(1,128)} %bitcast.12, f32[1,192]{1,0:T(1,128)} %bitcast.13, f32[1,192]{1,0:T(1,128)} %bitcast.14, f32[1,192]{1,0:T(1,128)} %bitcast.15, bf16[768]{0:T(1024)(128)(2,1)} %gain_ref.1, bf16[8,512]{1,0:T(8,128)(2,1)} %bitcast.10, bf16[8,512]{1,0:T(8,128)(2,1)} %bitcast.11, ...), custom_call_target="tpu_custom_call" | custom-call | tf_op jit(solution)/shard_map/pallas_call | solution.py:519
  132.9 1.1 copy.18
